TPU v7x, 32 devices: a whole 2x2x4 slice. The times are simulated.
32 devices in a mesh: section: 2 (over core), dp: 4 (over y, x), expert: 4 (over z).
Axes of the slice: x: 2, y: 2, z: 4, core: 2. Of those that a mesh axis runs over, the one named last changes fastest.
Arguments:
- tokens: bfloat16 [2, 64, 2048], P('section', 'expert'), may hold values from -6 to 6
- out_grad: bfloat16 [2, 64, 2048], P('section', 'expert'), may hold values from -6 to 6
- expert_ids: int32 [2, 64, 8], P('section', 'expert'), may hold values from 0 to 63, all different within a row; in each aligned block of 16 rows (0 to 15, 16 to 31, ..., all dimensions but the last counted through in order) at most 3 rows name the same one
- gates: bfloat16 [2, 64, 8], P('section', 'expert'), may hold values from 0.049804688 to 0.59765625
- w_gate: bfloat16 [2, 64, 2048, 1024], P('section', 'expert', None, 'dp'), may hold values from -0.125 to 0.125
- w_up: bfloat16 [2, 64, 2048, 1024], P('section', 'expert', None, 'dp'), may hold values from -0.125 to 0.125
- w_down: bfloat16 [2, 64, 1024, 2048], P('section', 'expert', 'dp'), may hold values from -0.1875 to 0.1875
Outputs:
- prev_grad: bfloat16 [2, 64, 2048], P('section', 'expert', 'dp')
- gate_grad: float32 [2, 64, 8], P('section', 'expert', 'dp')
- grad_w_gate: bfloat16 [2, 64, 2048, 1024], P('section', 'expert', None, 'dp')
- grad_w_up: bfloat16 [2, 64, 2048, 1024], P('section', 'expert', None, 'dp')
- grad_w_down: bfloat16 [2, 64, 1024, 2048], P('section', 'expert', 'dp')
Inputs may be any that keep to these rules, and one draw needn't show every extreme that they name: `expert_ids`: each token names 8 different experts; within one section, the 16 tokens of one index of expert name any one expert at most 3 times.
All inputs are finite; a program needn't handle non-finite values.
Results may differ from a plain program's by a relative error of at most 0.0057.
Values may be sent and summed in bfloat16 or wider, within the bound.
A program may use at most 192 MiB of HBM per device.

v0:
```python
import jax
import jax.numpy as jnp
from jax import lax
from jax.sharding import PartitionSpec as P

CAP = 3


def from_behind(value, axis, steps):
    count = lax.axis_size(axis)
    pairs = [(source, (source + steps) % count) for source in range(count)]
    return lax.ppermute(value, axis, pairs)


def expert_backward(xs, dys, gs, wg, wu, wd):
    a = jnp.dot(xs, wg, preferred_element_type=jnp.float32)
    b = jnp.dot(xs, wu, preferred_element_type=jnp.float32)
    sig = jax.nn.sigmoid(a)
    silu = a * sig
    hid = silu * b
    dz = jnp.dot(dys, wd.T, preferred_element_type=jnp.float32)
    gate_f = gs.astype(jnp.float32)[:, None]
    dgate = jnp.sum(hid * dz, axis=1)
    dh = gate_f * dz
    db = (dh * silu).astype(jnp.bfloat16)
    da = (dh * b * sig * (1.0 + a * (1.0 - sig))).astype(jnp.bfloat16)
    hid_b = hid.astype(jnp.bfloat16)
    dout = (gate_f * dys.astype(jnp.float32)).astype(jnp.bfloat16)
    dwg = jnp.dot(xs.T, da, preferred_element_type=jnp.float32)
    dwu = jnp.dot(xs.T, db, preferred_element_type=jnp.float32)
    dwd = jnp.dot(hid_b.T, dout, preferred_element_type=jnp.float32)
    dxp = jnp.dot(da, wg.T, preferred_element_type=jnp.float32) + jnp.dot(
        db, wu.T, preferred_element_type=jnp.float32
    )
    return (dxp, dgate, dwg, dwu, dwd)


def local(tokens, out_grad, expert_ids, gates, w_gate, w_up, w_down):
    x_local = tokens[0]
    dy_local = out_grad[0]
    ids = expert_ids[0]
    tok_dev, top = ids.shape
    n_exp = lax.axis_size("expert")
    exp_loc = w_gate.shape[1]
    experts = exp_loc * n_exp
    slots = experts * CAP
    flat = ids.reshape(-1)
    onehot = (flat[:, None] == jnp.arange(experts, dtype=jnp.int32)[None, :]).astype(jnp.int32)
    rank = jnp.sum((jnp.cumsum(onehot, axis=0) - onehot) * onehot, axis=1)
    slot_of = flat * CAP + rank
    pair_map = (slot_of[:, None] == jnp.arange(slots, dtype=jnp.int32)[None, :]).astype(jnp.float32)
    token_map = jnp.sum(pair_map.reshape(tok_dev, top, slots), axis=1)
    token_map_b = token_map.astype(jnp.bfloat16)
    gate_slots = jnp.dot(
        gates[0].reshape(-1).astype(jnp.float32), pair_map, precision=lax.Precision.HIGHEST
    ).astype(jnp.bfloat16)
    x_slots = jnp.dot(token_map_b.T, x_local, preferred_element_type=jnp.float32).astype(
        jnp.bfloat16
    )
    dy_slots = jnp.dot(token_map_b.T, dy_local, preferred_element_type=jnp.float32).astype(
        jnp.bfloat16
    )
    recv_x, recv_dy, recv_gate = (
        lax.all_to_all(x_slots, "expert", split_axis=0, concat_axis=0, tiled=True),
        lax.all_to_all(dy_slots, "expert", split_axis=0, concat_axis=0, tiled=True),
        lax.all_to_all(gate_slots, "expert", split_axis=0, concat_axis=0, tiled=True),
    )

    def to_experts(arr):
        rest = arr.shape[1:]
        shaped = arr.reshape((n_exp, exp_loc, CAP) + rest)
        return jnp.swapaxes(shaped, 0, 1).reshape((exp_loc, n_exp * CAP) + rest)

    def from_experts(arr):
        rest = arr.shape[2:]
        shaped = arr.reshape((exp_loc, n_exp, CAP) + rest)
        return jnp.swapaxes(shaped, 0, 1).reshape((slots,) + rest)

    def per_expert(operands):
        return expert_backward(*operands)

    dxp, dgp, dwg, dwu, dwd = lax.map(
        per_expert,
        (
            to_experts(recv_x),
            to_experts(recv_dy),
            to_experts(recv_gate),
            w_gate[0],
            w_up[0],
            w_down[0],
        ),
    )
    dx_slot = from_experts(dxp)
    dg_slot = from_experts(dgp)
    back_dx, back_dg = (
        lax.all_to_all(dx_slot, "expert", split_axis=0, concat_axis=0, tiled=True),
        lax.all_to_all(dg_slot, "expert", split_axis=0, concat_axis=0, tiled=True),
    )
    dx_full = jnp.dot(token_map, back_dx, precision=lax.Precision.HIGHEST)
    dg_pairs = jnp.dot(pair_map, back_dg, precision=lax.Precision.HIGHEST).reshape(tok_dev, top)
    dx_token, dg_token = (
        lax.psum_scatter(dx_full, "dp", scatter_dimension=1, tiled=True),
        lax.psum_scatter(dg_pairs, "dp", scatter_dimension=1, tiled=True),
    )
    arrived = from_behind(dx_token.astype(jnp.bfloat16), "section", -1)
    return (
        arrived[None],
        dg_token[None],
        dwg.astype(jnp.bfloat16)[None],
        dwu.astype(jnp.bfloat16)[None],
        dwd.astype(jnp.bfloat16)[None],
    )


def solution(mesh):
    placed = (
        P("section", "expert", None),
        P("section", "expert", None),
        P("section", "expert", None),
        P("section", "expert", None),
        P("section", "expert", None, "dp"),
        P("section", "expert", None, "dp"),
        P("section", "expert", "dp", None),
    )
    return jax.shard_map(
        local,
        mesh=mesh,
        in_specs=placed,
        out_specs=(
            P("section", "expert", "dp"),
            P("section", "expert", "dp"),
            P("section", "expert", None, "dp"),
            P("section", "expert", None, "dp"),
            P("section", "expert", "dp", None),
        ),
        check_vma=False,
    )
```

profile of v0, /device:TPU:0, one launch (start us, length us, event | category | flops | bytes accessed | tf_op | source)
XLA Modules:
  0.0 392.6 jit_solution(13189627752245280733)
XLA Ops:
  10.3 6.3 %all-to-all-start = ((bf16[4,48,1]{1,2,0:T(2,128)(2,1)}), bf16[4,48,1]{1,2,0:T(2,128)(2,1)S(1)}, u32[]{:S(2)}, u32[]{:S(2)}) async-start(bf16[4,48,1]{1,2,0:T(2,128)(2,1)} %all_to_all.46), calls=%async_computation | async-start | bytes 4096 | tf_op jit(solution)/shard_map/all_to_all | solution.py:66
  18.9 3.1 all-to-all-done
  22.1 3.5 all-to-all-start.1
  25.6 2.1 convolution_convert_fusion
  27.7 16.8 %all-to-all-done.1 = bf16[4,48,2048]{2,1,0:T(8,128)(2,1)S(1)} async-done(((bf16[4,48,2048]{2,1,0:T(8,128)(2,1)}), bf16[4,48,2048]{2,1,0:T(8,128)(2,1)S(1)}, u32[]{:S(2)}, u32[]{:S(2)}) %all-to-all-start.1) | async-done | bytes 786464 | tf_op jit(solution)/shard_map/all_to_all | solution.py:65
  44.5 3.5 all-to-all-start.2
  49.9 17.6 %all-to-all-done.2 = bf16[4,48,2048]{2,1,0:T(8,128)(2,1)S(1)} async-done(((bf16[4,48,2048]{2,1,0:T(8,128)(2,1)}), bf16[4,48,2048]{2,1,0:T(8,128)(2,1)S(1)}, u32[]{:S(2)}, u32[]{:S(2)}) %all-to-all-start.2) | async-done | bytes 786464 | tf_op jit(solution)/shard_map/all_to_all | solution.py:64
  69.1 247.2 %while.18 = (s32[]{:T(128)}, f32[16,12,2048]{2,0,1:T(8,128)}, f32[16,12]{1,0:T(8,128)S(1)}, bf16[16,2048,256]{2,1,0:T(8,128)(2,1)}, bf16[16,2048,256]{2,1,0:T(8,...) while((s32[]{:T(128)}, f32[16,12,2048]{2,0,1:T(8,128)}, ...), condition=%wide.region_5.6_spmd, body=%wide.region_3.5_spmd.sunk | while | flops 100832256 | bytes 12755305 | solution.py:82
  72.0 1.7 multiply_reduce_fusion.2
  78.1 1.6 fusion.102
  79.7 1.6 fusion.103
  81.5 3.0 dynamic_update_slice.30
  87.5 1.7 multiply_reduce_fusion.2
  93.6 1.6 fusion.102
  95.2 1.6 fusion.103
  96.9 3.0 dynamic_update_slice.30
  103.0 1.7 multiply_reduce_fusion.2
  110.6 1.6 fusion.103
  112.4 3.0 dynamic_update_slice.30
  118.4 1.7 multiply_reduce_fusion.2
  126.1 1.6 fusion.103
  127.8 3.0 dynamic_update_slice.30
  133.9 1.7 multiply_reduce_fusion.2
  141.5 1.6 fusion.103
  143.3 3.0 dynamic_update_slice.30
  149.3 1.7 multiply_reduce_fusion.2
  157.0 1.6 fusion.103
  158.7 3.0 dynamic_update_slice.30
  164.8 1.7 multiply_reduce_fusion.2
  172.5 1.6 fusion.103
  174.2 3.0 dynamic_update_slice.30
  180.2 1.7 multiply_reduce_fusion.2
  187.9 1.6 fusion.103
  189.6 3.0 dynamic_update_slice.30
  195.7 1.7 multiply_reduce_fusion.2
  203.4 1.6 fusion.103
  205.1 3.0 dynamic_update_slice.30
  211.1 1.7 multiply_reduce_fusion.2
  218.8 1.6 fusion.103
  220.5 3.0 dynamic_update_slice.30
  226.6 1.7 multiply_reduce_fusion.2
  234.2 1.6 fusion.103
  236.0 3.0 dynamic_update_slice.30
  242.0 1.7 multiply_reduce_fusion.2
  249.7 1.6 fusion.103
  251.4 3.0 dynamic_update_slice.30
  257.4 1.7 multiply_reduce_fusion.2
  265.1 1.6 fusion.103
  266.9 3.0 dynamic_update_slice.30
  272.9 1.7 multiply_reduce_fusion.2
  280.6 1.6 fusion.103
  282.3 3.0 dynamic_update_slice.30
  288.3 1.7 multiply_reduce_fusion.2
  296.0 1.6 fusion.103
  297.8 3.0 dynamic_update_slice.30
  303.8 1.7 multiply_reduce_fusion.2
  311.5 1.6 fusion.103
  313.2 3.0 dynamic_update_slice.30
  316.3 2.5 copy.88
  319.6 39.0 %all_to_all.52 = f32[4,48,2048]{2,1,0:T(8,128)S(1)} all-to-all(f32[4,48,2048]{2,1,0:T(8,128)S(1)} %copy.89), channel_id=1, replica_groups=mesh['section'=2,'dp'=4,'expert'=4] {'expert'}, dimensions={0} | all-to-all | bytes 3145728 | tf_op jit(solution)/shard_map/all_to_all | solution.py:96
  361.0 3.2 all-to-all-start.4
  365.5 4.2 %all-to-all-done.4 = f32[4,48,1]{1,2,0:T(1,128)S(1)} async-done(((f32[4,48,1]{1,2,0:T(1,128)}), f32[4,48,1]{1,2,0:T(1,128)S(1)}, u32[]{:S(2)}, u32[]{:S(2)}) %all-to-all-start.4) | async-done | bytes 800 | tf_op jit(solution)/shard_map/all_to_all | solution.py:97
  371.6 9.9 %all-reduce = f32[16,8]{0,1:T(8,128)S(1)} all-reduce(f32[16,8]{0,1:T(8,128)S(1)} %bitcast.168), channel_id=3, replica_groups=mesh['section'=2,'dp'=4,'expert'=4] {'dp'}, use_global_device_ids=true, to_apply=%region_7.8.clone | all-reduce | flops 128 | bytes 1024
  381.5 1.7 reduce-scatter.2.cloned.1.call-done
  (200 shorter events, 158.8 us)
Async XLA Ops:
  7.2 10.5 %copy-start = (bf16[1,16,2048]{2,1,0:T(8,128)(2,1)S(1)}, bf16[1,16,2048]{2,1,0:T(8,128)(2,1)}, u32[]{:S(2)}) copy-start(bf16[1,16,2048]{2,1,0:T(8,128)(2,1)} %param.10) | copy-start | bytes 196612
  10.3 11.8 %all-to-all-start = ((bf16[4,48,1]{1,2,0:T(2,128)(2,1)}), bf16[4,48,1]{1,2,0:T(2,128)(2,1)S(1)}, u32[]{:S(2)}, u32[]{:S(2)}) async-start(bf16[4,48,1]{1,2,0:T(2,128)(2,1)} %all_to_all.46), calls=%async_computation | async-start | bytes 4096 | tf_op jit(solution)/shard_map/all_to_all | solution.py:66
  22.1 22.4 %all-to-all-start.1 = ((bf16[4,48,2048]{2,1,0:T(8,128)(2,1)}), bf16[4,48,2048]{2,1,0:T(8,128)(2,1)S(1)}, u32[]{:S(2)}, u32[]{:S(2)}) async-start(bf16[4,48,2048]{2,1,0:T(8,128)(2,1)} %bitcast.16), calls=%async_computation.1 | async-start | bytes 1572864 | tf_op jit(solution)/shard_map/all_to_all | solution.py:65
  44.5 23.1 %all-to-all-start.2 = ((bf16[4,48,2048]{2,1,0:T(8,128)(2,1)}), bf16[4,48,2048]{2,1,0:T(8,128)(2,1)S(1)}, u32[]{:S(2)}, u32[]{:S(2)}) async-start(bf16[4,48,2048]{2,1,0:T(8,128)(2,1)} %bitcast.22), calls=%async_computation.2 | async-start | bytes 1572864 | tf_op jit(solution)/shard_map/all_to_all | solution.py:64
  48.0 335.2 %reduce-scatter.2.cloned.1.call-start = ((), (), s32[]{:S(2)}) async-start(), calls=%async_computation.6 | async-start | bytes 163840 | tf_op jit(solution)/shard_map/reduce_scatter | solution.py:102
  69.1 295.2 %copy-start.2 = (u32[32]{0:T(128)S(1)}, u32[32]{0:T(128)}, u32[]{:S(2)}) copy-start(u32[32]{0:T(128)} %constant.51) | copy-start | bytes 388
  316.3 69.5 %copy-start.1 = (bf16[1,16,2048]{2,1,0:T(8,128)(2,1)S(1)}, bf16[1,16,2048]{2,1,0:T(8,128)(2,1)}, u32[]{:S(2)}) copy-start(bf16[1,16,2048]{2,1,0:T(8,128)(2,1)} %param.10) | copy-start | bytes 196612
  361.0 8.7 %all-to-all-start.4 = ((f32[4,48,1]{1,2,0:T(1,128)}), f32[4,48,1]{1,2,0:T(1,128)S(1)}, u32[]{:S(2)}, u32[]{:S(2)}) async-start(f32[4,48,1]{1,2,0:T(1,128)} %bitcast.35), calls=%async_computation.5 | async-start | bytes 4096 | tf_op jit(solution)/shard_map/all_to_all | solution.py:97
  383.9 1.2 collective-permute-start
Sparse Core Ops, SparseCore 0:
  360.2 22.8 reduce-scatter.1
where the time goes:
time: 397 us; the launch traced here: 393 us
  matrix products  202 us (51%)
  local copies, waits for them, and re-layouts  63.3 us (16%)
  blocking collectives  48.9 us (12%)
  waiting for transfers between devices  44 us (11%)
  starting transfers between devices  16.6 us (4%)
  between operations  14.9 us (4%)
    dynamic_update_slice x48, local copies, waits for them, and re-layouts, local(): lax.map(per_expert, (to_experts(recv_x), to_experts(recv_dy), to_experts(...  50.7 us
    all_to_all x1, blocking collectives, local(): lax.all_to_all(dx_slot, 'expert', split_axis=0, concat_axis=0, tiled=True)  39 us
    dot_general x16, matrix products, expert_backward(): dz = jnp.dot(dys, wd.T, preferred_element_type=jnp.float32)  27.7 us
    dot_general x16, matrix products, expert_backward(): jnp.dot(db, wu.T, preferred_element_type=jnp.float32)  25.8 us
    dot_general x16, matrix products, expert_backward(): jnp.dot(da, wg.T, preferred_element_type=jnp.float32)  25.5 us
    dot_general x16, matrix products, expert_backward(): b = jnp.dot(xs, wu, preferred_element_type=jnp.float32)  23.6 us
    dot_general x16, matrix products, expert_backward(): a = jnp.dot(xs, wg, preferred_element_type=jnp.float32)  23.6 us
    dot_general x16, matrix products, expert_backward(): dwg = jnp.dot(xs.T, da, preferred_element_type=jnp.float32)  23.4 us
  transfers between devices with their start and end apart: 6, of which 6 were waited for; matrix products, arithmetic and copies ran while one was open for 2% of the time, Pallas kernels for 0%

commit v1 on v0

--- a/solution.py
+++ b/solution.py
@@ -4,6 +4,29 @@
 from jax.sharding import PartitionSpec as P
 
 CAP = 3
+
+
+def cut_along(x, dim, size):
+    lengths = x.shape
+    parts = x.reshape(*lengths[:dim], size, lengths[dim] // size, *lengths[dim + 1 :])
+    return jnp.moveaxis(parts, dim, 0)
+
+
+def laid_out(parts, dim):
+    parts = jnp.moveaxis(parts, 0, dim)
+    lengths = parts.shape
+    return parts.reshape(*lengths[:dim], lengths[dim] * lengths[dim + 1], *lengths[dim + 2 :])
+
+
+def exchange_directly(array, axis, split_dim, concat_dim):
+    size, here = (lax.axis_size(axis), lax.axis_index(axis))
+    parts = cut_along(array, split_dim, size)
+    outs = [parts[here]]
+    for hop in range(1, size):
+        sent = parts[(here + hop) % size]
+        outs.append(lax.ppermute(sent, axis, [(i, (i + hop) % size) for i in range(size)]))
+    parts = jnp.stack(outs)[(here - jnp.arange(size)) % size]
+    return laid_out(parts, concat_dim)
 
 
 def from_behind(value, axis, steps):
@@ -61,7 +84,7 @@
         jnp.bfloat16
     )
     recv_x, recv_dy, recv_gate = (
-        lax.all_to_all(x_slots, "expert", split_axis=0, concat_axis=0, tiled=True),
+        exchange_directly(x_slots, "expert", 0, 0),
         lax.all_to_all(dy_slots, "expert", split_axis=0, concat_axis=0, tiled=True),
         lax.all_to_all(gate_slots, "expert", split_axis=0, concat_axis=0, tiled=True),
     )

time: 397 us -> 392 us (0.987)
  waiting for transfers between devices: 44 us -> 34.8 us
    ppermute x0 -> x3, waiting for transfers between devices: none -> 25.1 us  [exchange_directly(): lax.ppermute(sent, axis, [(i, (i + hop) % size) for i in range(size)])]
    all_to_all x1 -> x0, waiting for transfers between devices: 17.6 us -> none  [local(): lax.all_to_all(x_slots, 'expert', split_axis=0, concat_axis=0, tiled=True)]
    all_to_all x1, waiting for transfers between devices: 16.8 us -> 0.01 us  [local(): lax.all_to_all(dy_slots, 'expert', split_axis=0, concat_axis=0, tiled=True)]
    ppermute x0 -> x3, starting transfers between devices: none -> 5.77 us  [exchange_directly(): lax.ppermute(sent, axis, [(i, (i + hop) % size) for i in range(size)])]
  transfers between devices with their start and end apart: 6 -> 8, of which waited for: 6 -> 6; matrix products, arithmetic and copies ran while one was open for 2% -> 2% of each run, Pallas kernels for 0% -> 0%
where the time goes in v1:
time: 392 us; the launch traced here: 388 us
  matrix products  201 us (51%)
  local copies, waits for them, and re-layouts  64 us (16%)
  blocking collectives  50.9 us (13%)
  waiting for transfers between devices  34.8 us (9%)
  starting transfers between devices  18.8 us (5%)
  between operations  14.9 us (4%)
    dynamic_update_slice x48, local copies, waits for them, and re-layouts, local(): lax.map(per_expert, (to_experts(recv_x), to_experts(recv_dy), to_experts(...  50.7 us
    all_to_all x1, blocking collectives, local(): lax.all_to_all(dx_slot, 'expert', split_axis=0, concat_axis=0, tiled=True)  41 us
    dot_general x16, matrix products, expert_backward(): dz = jnp.dot(dys, wd.T, preferred_element_type=jnp.float32)  27.7 us
    dot_general x16, matrix products, expert_backward(): jnp.dot(db, wu.T, preferred_element_type=jnp.float32)  25.8 us
    dot_general x16, matrix products, expert_backward(): jnp.dot(da, wg.T, preferred_element_type=jnp.float32)  25.5 us
    ppermute x3, waiting for transfers between devices, exchange_directly(): lax.ppermute(sent, axis, [(i, (i + hop) % size) for i in range(size)])  25.1 us
    dot_general x16, matrix products, expert_backward(): a = jnp.dot(xs, wg, preferred_element_type=jnp.float32)  23.6 us
    dot_general x16, matrix products, expert_backward(): b = jnp.dot(xs, wu, preferred_element_type=jnp.float32)  23.6 us
  transfers between devices with their start and end apart: 8, of which 6 were waited for; matrix products, arithmetic and copies ran while one was open for 2% of the time, Pallas kernels for 0%

profile of v1, /device:TPU:0, one launch (start us, length us, event | category | flops | bytes accessed | tf_op | source)
XLA Modules:
  0.0 387.5 jit_solution(3972315570855143757)
XLA Ops:
  10.3 6.3 %all-to-all-start = ((bf16[4,48,1]{1,2,0:T(2,128)(2,1)}), bf16[4,48,1]{1,2,0:T(2,128)(2,1)S(1)}, u32[]{:S(2)}, u32[]{:S(2)}) async-start(bf16[4,48,1]{1,2,0:T(2,128)(2,1)} %all_to_all.38), calls=%async_computation | async-start | bytes 4096 | tf_op jit(solution)/shard_map/all_to_all | solution.py:89
  18.9 3.1 all-to-all-done
  22.1 3.5 all-to-all-start.1
  27.0 1.9 collective-permute-start
  28.9 2.4 collective-permute-start.1
  33.1 14.9 %collective-permute-done = bf16[48,2048]{1,0:T(8,128)(2,1)S(1)} collective-permute-done((bf16[48,2048]{1,0:T(8,128)(2,1)S(1)}, bf16[48,2048]{1,0:T(8,128)(2,1)S(1)}, u32[]{:S(2)}, u32[]{:S(2)}) %collective-permute-start) | collective-permute-done | bytes 196640 | tf_op jit(solution)/shard_map/ppermute | solution.py:27
  48.0 10.2 %collective-permute-done.1 = bf16[48,2048]{1,0:T(8,128)(2,1)S(1)} collective-permute-done((bf16[48,2048]{1,0:T(8,128)(2,1)S(1)}, bf16[48,2048]{1,0:T(8,128)(2,1)S(1)}, u32[]{:S(2)}, u32[]{:S(2)}) %collective-permute-start.1) | collective-permute-done | bytes 196640 | tf_op jit(solution)/shard_map/ppermute | solution.py:27
  62.0 247.2 %while.18 = (s32[]{:T(128)}, f32[16,12,2048]{2,0,1:T(8,128)}, f32[16,12]{1,0:T(8,128)S(1)}, bf16[16,2048,256]{2,1,0:T(8,128)(2,1)}, bf16[16,2048,256]{2,1,0:T(8,...) while((s32[]{:T(128)}, f32[16,12,2048]{2,0,1:T(8,128)}, ...), condition=%wide.region_5.6_spmd, body=%wide.region_3.5_spmd.sunk | while | flops 100832256 | bytes 12755305 | solution.py:105
  64.9 1.7 multiply_reduce_fusion.2
  71.0 1.6 fusion.104
  72.6 1.6 fusion.105
  74.4 3.0 dynamic_update_slice.30
  80.4 1.7 multiply_reduce_fusion.2
  86.5 1.6 fusion.104
  88.1 1.6 fusion.105
  89.8 3.0 dynamic_update_slice.30
  95.8 1.7 multiply_reduce_fusion.2
  103.5 1.6 fusion.105
  105.3 3.0 dynamic_update_slice.30
  111.3 1.7 multiply_reduce_fusion.2
  119.0 1.6 fusion.105
  120.7 3.0 dynamic_update_slice.30
  126.7 1.7 multiply_reduce_fusion.2
  134.4 1.6 fusion.105
  136.2 3.0 dynamic_update_slice.30
  142.2 1.7 multiply_reduce_fusion.2
  149.9 1.6 fusion.105
  151.6 3.0 dynamic_update_slice.30
  157.6 1.7 multiply_reduce_fusion.2
  165.3 1.6 fusion.105
  167.1 3.0 dynamic_update_slice.30
  173.1 1.7 multiply_reduce_fusion.2
  180.8 1.6 fusion.105
  182.5 3.0 dynamic_update_slice.30
  188.6 1.7 multiply_reduce_fusion.2
  196.2 1.6 fusion.105
  198.0 3.0 dynamic_update_slice.30
  204.0 1.7 multiply_reduce_fusion.2
  211.7 1.6 fusion.105
  213.4 3.0 dynamic_update_slice.30
  219.4 1.7 multiply_reduce_fusion.2
  227.1 1.6 fusion.105
  228.9 3.0 dynamic_update_slice.30
  234.9 1.7 multiply_reduce_fusion.2
  242.6 1.6 fusion.105
  244.3 3.0 dynamic_update_slice.30
  250.3 1.7 multiply_reduce_fusion.2
  258.0 1.6 fusion.105
  259.8 3.0 dynamic_update_slice.30
  265.8 1.7 multiply_reduce_fusion.2
  273.5 1.6 fusion.105
  275.2 3.0 dynamic_update_slice.30
  281.2 1.7 multiply_reduce_fusion.2
  288.9 1.6 fusion.105
  290.6 3.0 dynamic_update_slice.30
  296.7 1.7 multiply_reduce_fusion.2
  304.3 1.6 fusion.105
  306.1 3.0 dynamic_update_slice.30
  309.1 2.5 copy.87
  312.5 41.0 %all_to_all.43 = f32[4,48,2048]{2,1,0:T(8,128)S(1)} all-to-all(f32[4,48,2048]{2,1,0:T(8,128)S(1)} %copy.88), channel_id=1, replica_groups=mesh['section'=2,'dp'=4,'expert'=4] {'expert'}, dimensions={0} | all-to-all | bytes 3145728 | tf_op jit(solution)/shard_map/all_to_all | solution.py:119
  355.9 3.2 all-to-all-start.3
  360.4 4.2 %all-to-all-done.3 = f32[4,48,1]{1,2,0:T(1,128)S(1)} async-done(((f32[4,48,1]{1,2,0:T(1,128)}), f32[4,48,1]{1,2,0:T(1,128)S(1)}, u32[]{:S(2)}, u32[]{:S(2)}) %all-to-all-start.3) | async-done | bytes 800 | tf_op jit(solution)/shard_map/all_to_all | solution.py:120
  366.5 9.9 %all-reduce = f32[16,8]{0,1:T(8,128)S(1)} all-reduce(f32[16,8]{0,1:T(8,128)S(1)} %bitcast.183), channel_id=3, replica_groups=mesh['section'=2,'dp'=4,'expert'=4] {'dp'}, use_global_device_ids=true, to_apply=%region_7.8.clone | all-reduce | flops 128 | bytes 1024
  376.4 1.8 reduce-scatter.2.cloned.1.call-done
  (209 shorter events, 162.3 us)
Async XLA Ops:
  7.2 10.5 %copy-start = (bf16[1,16,2048]{2,1,0:T(8,128)(2,1)S(1)}, bf16[1,16,2048]{2,1,0:T(8,128)(2,1)}, u32[]{:S(2)}) copy-start(bf16[1,16,2048]{2,1,0:T(8,128)(2,1)} %param.10) | copy-start | bytes 196612
  10.3 11.8 %all-to-all-start = ((bf16[4,48,1]{1,2,0:T(2,128)(2,1)}), bf16[4,48,1]{1,2,0:T(2,128)(2,1)S(1)}, u32[]{:S(2)}, u32[]{:S(2)}) async-start(bf16[4,48,1]{1,2,0:T(2,128)(2,1)} %all_to_all.38), calls=%async_computation | async-start | bytes 4096 | tf_op jit(solution)/shard_map/all_to_all | solution.py:89
  22.1 38.4 %all-to-all-start.1 = ((bf16[4,48,2048]{2,1,0:T(8,128)(2,1)}), bf16[4,48,2048]{2,1,0:T(8,128)(2,1)S(1)}, u32[]{:S(2)}, u32[]{:S(2)}) async-start(bf16[4,48,2048]{2,1,0:T(8,128)(2,1)} %bitcast.16), calls=%async_computation.1 | async-start | bytes 1572864 | tf_op jit(solution)/shard_map/all_to_all | solution.py:88
  25.6 352.6 %reduce-scatter.2.cloned.1.call-start = ((), (), s32[]{:S(2)}) async-start(), calls=%async_computation.5 | async-start | bytes 163840 | tf_op jit(solution)/shard_map/reduce_scatter | solution.py:125
  27.0 21.1 %collective-permute-start = (bf16[48,2048]{1,0:T(8,128)(2,1)S(1)}, bf16[48,2048]{1,0:T(8,128)(2,1)S(1)}, u32[]{:S(2)}, u32[]{:S(2)}) collective-permute-start(bf16[48,2048]{1,0:T(8,128)(2,1)S(1)} %get-tuple-element.154), channel_id=1, source_target_pairs={{0,1},{1,2},{2,3},{3,0},{4,5},{5,6},{6,7},{7,4},{8,9},{9,10},{10,1... | collective-permute-start | bytes 589832 | tf_op jit(solution)/shard_map/ppermute | solution.py:27
  28.9 29.3 %collective-permute-start.1 = (bf16[48,2048]{1,0:T(8,128)(2,1)S(1)}, bf16[48,2048]{1,0:T(8,128)(2,1)S(1)}, u32[]{:S(2)}, u32[]{:S(2)}) collective-permute-start(bf16[48,2048]{1,0:T(8,128)(2,1)S(1)} %get-tuple-element.153), channel_id=1, source_target_pairs={{0,2},{1,3},{2,0},{3,1},{4,6},{5,7},{6,4},{7,5},{8,10},{9,11},{10,... | collective-permute-start | bytes 589832 | tf_op jit(solution)/shard_map/ppermute | solution.py:27
  31.3 26.9 %collective-permute-start.2 = (bf16[48,2048]{1,0:T(8,128)(2,1)S(1)}, bf16[48,2048]{1,0:T(8,128)(2,1)S(1)}, u32[]{:S(2)}, u32[]{:S(2)}) collective-permute-start(bf16[48,2048]{1,0:T(8,128)(2,1)S(1)} %get-tuple-element.152), channel_id=1, source_target_pairs={{0,3},{1,0},{2,1},{3,2},{4,7},{5,4},{6,5},{7,6},{8,11},{9,8},{10,9... | collective-permute-start | bytes 589832 | tf_op jit(solution)/shard_map/ppermute | solution.py:27
  61.9 297.2 %copy-start.2 = (u32[32]{0:T(128)S(1)}, u32[32]{0:T(128)}, u32[]{:S(2)}) copy-start(u32[32]{0:T(128)} %constant.89) | copy-start | bytes 388
  309.1 71.6 %copy-start.1 = (bf16[1,16,2048]{2,1,0:T(8,128)(2,1)S(1)}, bf16[1,16,2048]{2,1,0:T(8,128)(2,1)}, u32[]{:S(2)}) copy-start(bf16[1,16,2048]{2,1,0:T(8,128)(2,1)} %param.10) | copy-start | bytes 196612
  355.9 8.7 %all-to-all-start.3 = ((f32[4,48,1]{1,2,0:T(1,128)}), f32[4,48,1]{1,2,0:T(1,128)S(1)}, u32[]{:S(2)}, u32[]{:S(2)}) async-start(f32[4,48,1]{1,2,0:T(1,128)} %bitcast.42), calls=%async_computation.4 | async-start | bytes 4096 | tf_op jit(solution)/shard_map/all_to_all | solution.py:120
  378.9 1.2 collective-permute-start.3
Sparse Core Ops, SparseCore 0:
  355.1 22.9 reduce-scatter.1
